TPU v7x, 512 devices: a whole 4x4x16 slice. The times are simulated.
512 devices in a mesh: leaf: 128 (over z, x, core), rep: 4 (over y).
Axes of the slice: x: 4, y: 4, z: 16, core: 2. Of those that a mesh axis runs over, the one named last changes fastest.
Arguments:
- ancestors: bfloat16 [3072, 3072], P('leaf', 'rep'), may hold values from -6 to 6
- panels: bfloat16 [128, 1024, 512], P('leaf'), may hold values from -0.1875 to 0.1875
- structure: int32 [128, 4], P('leaf'), may hold values from 0 to 11, as said below
- inverse_diag: float32 [128, 512, 512], P('leaf', 'rep'), may hold values from -6 to 6
Outputs:
- offdiag: bfloat16 [128, 1024, 512], P('leaf', 'rep')
- diag: float32 [128, 512, 512], P('leaf', 'rep')
Inputs may be any that keep to these rules, and one draw needn't show every extreme that they name: `structure`: each row holds 4 different ancestor block numbers in increasing order.
All inputs are finite; a program needn't handle non-finite values.
Results may differ from a plain program's by a relative error of at most 0.012.
Values may be sent and summed in bfloat16 or wider, within the bound.
A program may use at most 64 MiB of HBM per device.

v0:
```python
import jax
import jax.numpy as jnp
from jax import lax
from jax.sharding import PartitionSpec as P


def per_device(ancestors, panels, structure, inverse_diag):
    children = panels.shape[0]
    entries = structure.shape[1]
    block_width = panels.shape[1] // entries
    child_width = panels.shape[2]
    quarter = ancestors.shape[1]
    blocks_here = quarter // block_width
    replica = lax.axis_index("rep")
    replicas = lax.axis_size("rep")
    row_share = entries * block_width // replicas
    child_ids = jnp.arange(children, dtype=jnp.int32)
    first_block = replica * blocks_here
    local_ids = first_block + jnp.arange(blocks_here, dtype=jnp.int32)
    matches = (structure[:, None, :] == local_ids[None, :, None]).astype(jnp.bfloat16)
    panel_blocks = panels.reshape(children, entries, block_width, child_width)
    local_panel = jnp.einsum(
        "cbs,cswk->cbwk", matches, panel_blocks, preferred_element_type=jnp.float32
    ).astype(jnp.bfloat16)
    right_side = local_panel.transpose(1, 2, 0, 3).reshape(quarter, children * child_width)
    gathered = -jnp.dot(
        lax.all_gather(ancestors, "leaf", axis=0, tiled=True),
        right_side,
        preferred_element_type=jnp.float32,
    )
    total_blocks = gathered.shape[0] // block_width
    gathered = gathered.reshape(total_blocks, block_width, children, child_width)
    partial_value = gathered[structure, :, child_ids[:, None], :]
    partial_value = partial_value.reshape(children, entries * block_width, child_width)
    summed = lax.psum_scatter(partial_value, "rep", scatter_dimension=1, tiled=True)
    offdiag = summed.astype(jnp.bfloat16)
    panel_share = lax.dynamic_slice_in_dim(panels, replica * row_share, row_share, 1)
    diag_terms = jnp.einsum(
        "crk,crl->ckl", panel_share, offdiag, preferred_element_type=jnp.float32
    )
    diag_share = lax.psum_scatter(
        diag_terms.astype(jnp.bfloat16), "rep", scatter_dimension=1, tiled=True
    ).astype(jnp.float32)
    diag = inverse_diag - diag_share
    return (offdiag, diag)


def solution(mesh):
    return jax.shard_map(
        per_device,
        mesh=mesh,
        in_specs=(P("leaf", "rep"), P("leaf", None, None), P("leaf", None), P("leaf", "rep", None)),
        out_specs=(P("leaf", "rep", None), P("leaf", "rep", None)),
        check_vma=False,
    )
```

profile of v0, /device:TPU:1, one launch (start us, length us, event | category | flops | bytes accessed | tf_op | source)
XLA Modules:
  0.0 248.9 jit_solution(12309326673819076844)
XLA Ops:
  7.2 0.0 copy-start
  7.2 0.0 all-gather.2.cloned.1.call-start
  7.2 0.7 all-gather.2.cloned.1.call-update
  7.9 0.0 reduce-scatter.3.cloned.1.call-start
  8.0 0.4 copy-done
  8.4 1.6 convolution_convert_fusion
  10.0 0.2 copy.9
  10.2 0.7 fusion.9
  10.9 148.8 %all-gather.2.cloned.1.call-done = bf16[3072,768]{1,0:T(8,128)(2,1)} async-done(((bf16[24,768]{1,0:T(8,128)(2,1)}), bf16[3072,768]{1,0:T(8,128)(2,1)}) %all-gather.2.cloned.1.call-update) | async-done | bytes 4718608 | tf_op jit(solution)/shard_map/all_gather | solution.py:27
  159.7 6.9 %negate_bitcast_fusion = f32[3072,512]{0,1:T(8,128)} fusion(bf16[768,512]{1,0:T(8,128)(2,1)S(1)} %bitcast.31, bf16[3072,768]{1,0:T(8,128)(2,1)} %all-gather.2.cloned.1.call-done), kind=kOutput, calls=%fused_computation.1 | convolution fusion | flops 2417491968 | bytes 11796480 | tf_op jit(solution)/shard_map/dot_general | solution.py:26
  166.6 6.6 %copy.10 = f32[3072,512]{1,0:T(8,128)} copy(f32[3072,512]{0,1:T(8,128)} %negate_bitcast_fusion) | data formatting | bytes 12582912 | tf_op jit(solution)/shard_map/neg | solution.py:26
  173.1 0.0 copy-start.2
  173.1 4.9 %gather_fusion = f32[4,256,512]{2,1,0:T(8,128)} fusion(f32[12,256,1,512]{3,1,2,0:T(8,128)} %bitcast.29, s32[4]{0:T(128)S(1)} %or_bitcast_fusion), kind=kCustom, calls=%fused_computation | custom fusion | bytes 4194336 | tf_op jit(solution)/shard_map/gather | solution.py:33
  178.0 0.0 reduce-scatter.3.cloned.1.call-update
  178.0 0.0 reduce-scatter.5.cloned.1.call-start
  178.1 32.4 %reduce-scatter.3.cloned.1.call-done = f32[1,256,512]{2,1,0:T(8,128)} async-done(((f32[1,1024,512]{2,1,0:T(8,128)}), f32[1,256,512]{2,1,0:T(8,128)}) %reduce-scatter.3.cloned.1.call-update) | async-done | bytes 524304 | tf_op jit(solution)/shard_map/reduce_scatter | solution.py:35
  210.4 1.1 convert_element_type.18
  211.5 0.0 copy-start.1
  211.5 1.1 fusion
  212.7 0.0 reduce-scatter.5.cloned.1.call-update
  212.7 28.0 %reduce-scatter.5.cloned.1.call-done = bf16[1,128,512]{2,1,0:T(8,128)(2,1)} async-done(((bf16[1,512,512]{2,1,0:T(8,128)(2,1)}), bf16[1,128,512]{2,1,0:T(8,128)(2,1)}) %reduce-scatter.5.cloned.1.call-update) | async-done | bytes 131088 | tf_op jit(solution)/shard_map/reduce_scatter | solution.py:41
  240.7 0.0 copy-done.2
  240.7 1.6 convert_subtract_fusion
  242.4 0.0 copy-done.1
  (3 shorter events, 0.0 us)
Async XLA Ops:
  7.2 1.2 copy-start
  7.2 152.5 %all-gather.2.cloned.1.call-start = ((), (), s32[]{:S(2)}) async-start(), calls=%async_computation.2 | async-start | bytes 4755456 | tf_op jit(solution)/shard_map/all_gather | solution.py:27
  7.9 202.5 %reduce-scatter.3.cloned.1.call-start = ((), (), s32[]{:S(2)}) async-start(), calls=%async_computation.3 | async-start | bytes 2621440 | tf_op jit(solution)/shard_map/reduce_scatter | solution.py:35
  173.1 67.6 %copy-start.2 = (f32[1,128,512]{2,1,0:T(8,128)S(1)}, f32[1,128,512]{2,1,0:T(8,128)}, u32[]{:S(2)}) copy-start(f32[1,128,512]{2,1,0:T(8,128)} %param.7) | copy-start | bytes 786436
  178.0 62.7 %reduce-scatter.5.cloned.1.call-start = ((), (), s32[]{:S(2)}) async-start(), calls=%async_computation.4 | async-start | bytes 655360 | tf_op jit(solution)/shard_map/reduce_scatter | solution.py:41
  211.5 30.8 %copy-start.1 = (bf16[1,256,512]{2,1,0:T(8,128)(2,1)}, bf16[1,256,512]{2,1,0:T(8,128)(2,1)S(1)}, u32[]{:S(2)}) copy-start(bf16[1,256,512]{2,1,0:T(8,128)(2,1)S(1)} %convert_element_type.18) | copy-start | bytes 786436
Sparse Core Ops, SparseCore 0:
  11.1 148.5 all-gather.1
  178.1 32.2 reduce-scatter.2
  213.5 27.1 reduce-scatter.4
where the time goes:
time: 250 us; the launch traced here: 249 us
  waiting for transfers between devices  210 us (84%)
  between operations  13.8 us (6%)
  local copies, waits for them, and re-layouts  12 us (5%)
  matrix products  9.66 us (4%)
  other arithmetic  3.38 us (1%)
    all_gather x1, waiting for transfers between devices, per_device(): lax.all_gather(ancestors, 'leaf', axis=0, tiled=True)  149 us
    reduce_scatter x1, waiting for transfers between devices, per_device(): lax.psum_scatter(partial_value, 'rep', scatter_dimension=1, tiled=True)  32.4 us
    reduce_scatter x1, waiting for transfers between devices, per_device(): lax.psum_scatter(diag_terms.astype(jnp.bfloat16), 'rep', scatter_dimensio...  28 us
    dot_general x1, matrix products, per_device(): jnp.dot(lax.all_gather(ancestors, 'leaf', axis=0, tiled=True), right_side...  6.92 us
    neg x1, local copies, waits for them, and re-layouts, per_device(): -jnp.dot(lax.all_gather(ancestors, 'leaf', axis=0, tiled=True), right_sid...  6.55 us
  transfers between devices with their start and end apart: 3, of which 3 were waited for; matrix products, arithmetic and copies ran while one was open for 1% of the time, Pallas kernels for 0%

commit v1 on v0

v1 whole, which is shorter than its diff:
```python
import jax
import jax.numpy as jnp
from jax import lax
from jax.experimental import pallas as pl
from jax.experimental.pallas import tpu as pltpu
from jax.sharding import PartitionSpec as P

MESH = pl.DeviceIdType.MESH
Z, X, Y, CORES = 16, 4, 4, 2
PLANE = X * Y * CORES
GROUPS = 3
F32, BF16 = jnp.float32, jnp.bfloat16


def kernel(
    anc_ref, struct_ref, panels_hbm, inv_hbm, off_hbm, diag_hbm,
    panels, inv, s0_send, s0_recv, st_send, st_all, st_smem, tiles, stage, picked, lhs, pt,
    off, d_send, d_recv, diag,
    in_sem, out_sem, s0_sems, st_sems, ring_send, ring_recv, pick_sems, d_send_sem, d_recv_sem,
):
    me, y = lax.axis_index("leaf"), lax.axis_index("rep")
    z, x, c = me // 8, (me // 2) % 4, me % 2

    def leaf(zz, xx, cc):
        return (zz * X + xx) * CORES + cc

    get_panels = pltpu.make_async_copy(panels_hbm.at[0], panels, in_sem.at[0])
    get_inv = pltpu.make_async_copy(inv_hbm.at[0], inv, in_sem.at[1])
    get_panels.start()
    get_inv.start()

    barrier = pltpu.get_barrier_semaphore()

    def greet(n, carry):
        there = leaf(z, (x + n // 8) % X, (c + n % 2) % CORES)
        pl.semaphore_signal(barrier, inc=1, device_id=(there, (y + n // 2) % Y), device_id_type=MESH)
        return carry

    lax.fori_loop(1, PLANE, greet, 0)
    up, down = leaf((z + 1) % Z, x, c), leaf((z + Z - 1) % Z, x, c)
    for there in (up, down):
        pl.semaphore_signal(barrier, inc=1, device_id=(there, y), device_id_type=MESH)

    rows = anc_ref[...].astype(F32)
    for h in range(3):
        for k in range(CORES):
            for t in range(3):
                s0_send[h, k, t] = rows[8 * h:8 * h + 8, 256 * t + 128 * k:256 * t + 128 * k + 128]
    lane = lax.broadcasted_iota(jnp.int32, (8, 128), 1)
    blocks = jnp.zeros((8, 128), jnp.int32)
    for q in range(4):
        blocks = jnp.where(lane == q, struct_ref[0, q], blocks)
    slot = 2 * x + c
    st_send[...] = blocks
    st_all[slot] = blocks

    pl.semaphore_wait(barrier, PLANE + 1)

    for h in range(3):
        eighth = 6 * x + 3 * c + h
        group, half = eighth // 2, eighth % 2
        entry, to_x = group // 4, group % 4
        to_y = (3 * z + entry + y) % Y
        for k in range(CORES):
            here = jnp.logical_and(jnp.logical_and(to_x == x, to_y == y), c == k)

            @pl.when(here)
            def _():
                pltpu.make_async_copy(s0_send.at[h, k], s0_recv.at[entry, half], s0_sems.at[1]).start()

            @pl.when(jnp.logical_not(here))
            def _():
                pltpu.make_async_remote_copy(
                    src_ref=s0_send.at[h, k], dst_ref=s0_recv.at[entry, half],
                    send_sem=s0_sems.at[2 + 2 * h + k], recv_sem=s0_sems.at[1],
                    device_id=(leaf(z, to_x, k), to_y), device_id_type=MESH,
                ).start()

    def tell(n, carry):
        pltpu.make_async_remote_copy(
            src_ref=st_send, dst_ref=st_all.at[slot], send_sem=st_sems.at[0], recv_sem=st_sems.at[1],
            device_id=(leaf(z, (x + n // 2) % X, (c + n % 2) % CORES), y), device_id_type=MESH,
        ).start()
        return carry

    lax.fori_loop(1, X * CORES, tell, 0)

    pltpu.make_async_copy(s0_recv, s0_recv, s0_sems.at[1]).wait()
    for e in range(GROUPS):
        for t in range(3):
            both = jnp.concatenate([s0_recv[e, 0, t], s0_recv[e, 1, t]], axis=0)
            tiles[GROUPS * z + e, t] = both.astype(BF16)

    def pass_on(way, step, e):
        origin = (z + Z - step) % Z if way == 0 else (z + step) % Z
        part = tiles.at[GROUPS * origin + e]
        return pltpu.make_async_remote_copy(
            src_ref=part, dst_ref=part, send_sem=ring_send, recv_sem=ring_recv.at[way, step, e],
            device_id=(up if way == 0 else down, y), device_id_type=MESH,
        )

    def arrived(way, step, e):
        part = tiles.at[0]
        pltpu.make_async_copy(part, part, ring_recv.at[way, step, e]).wait()

    for e in range(GROUPS):
        pass_on(0, 0, e).start()
        pass_on(1, 0, e).start()

    get_panels.wait()
    pt[...] = panels[pl.ds(pl.multiple_of(256 * y, 256), 256), :].T
    told = st_all.at[pl.ds(0, X * CORES - 1)]
    pltpu.make_async_copy(told, told, st_sems.at[1]).wait()
    to_smem = pltpu.make_async_copy(st_all, st_smem, in_sem.at[2])
    to_smem.start()

    for step in range(1, Z // 2 - 1):
        for e in range(GROUPS):
            for way in range(2):
                arrived(way, step - 1, e)
                pass_on(way, step, e).start()
    for e in range(GROUPS):
        for way in range(2):
            arrived(way, Z // 2 - 2, e)

            @pl.when(c == way)
            def _():
                pass_on(way, Z // 2 - 1, e).start()

    to_smem.wait()
    for e in range(GROUPS):
        for way in range(2):

            @pl.when(c == way)
            def _():
                arrived(way, Z // 2 - 1, e)

    def pick(n, to_x, to_c, to_y):
        child = 2 * to_x + to_c
        row = st_smem[child, 0, to_y]
        for q in range(4):
            column = st_smem[child, 0, q]
            held = 4 * row + lax.rem(y + 4 - lax.div(column, 3), 4)
            stage[n, q] = tiles[held, lax.rem(column, 3)]

    def send(n, carry):
        to_x, to_c, to_y = (x + n // 8) % X, (c + n % 2) % CORES, (y + n // 2) % Y
        pick(n, to_x, to_c, to_y)
        pltpu.make_async_remote_copy(
            src_ref=stage.at[n], dst_ref=picked.at[c, y, x], send_sem=pick_sems.at[0], recv_sem=pick_sems.at[1],
            device_id=(leaf(z, to_x, to_c), to_y), device_id_type=MESH,
        ).start()
        return carry

    lax.fori_loop(1, PLANE, send, 0)
    pick(0, x, c, y)
    pltpu.make_async_copy(stage.at[0], picked.at[c, y, x], pick_sems.at[1]).start()

    pltpu.make_async_copy(picked, picked, pick_sems.at[1]).wait()

    for q in range(4):
        quarter = lax.div(struct_ref[0, q], 3)
        for k in range(CORES):
            for part in range(4):
                rows64 = picked[k, lax.rem(quarter + part, 4), :, q]
                lhs[64 * part:64 * part + 64, 256 * q + 128 * k:256 * q + 128 * k + 128] = rows64.reshape(64, 128)
    off[...] = (-jnp.dot(lhs[...], panels[...], preferred_element_type=F32)).astype(BF16)
    put_off = pltpu.make_async_copy(off, off_hbm.at[0], out_sem.at[0])
    put_off.start()

    def share(r):
        return jnp.dot(pt[pl.ds(pl.multiple_of(128 * r, 128), 128), :], off[...], preferred_element_type=F32)

    def give(j):
        return pltpu.make_async_remote_copy(
            src_ref=d_send.at[j], dst_ref=d_recv.at[j], send_sem=d_send_sem.at[j], recv_sem=d_recv_sem.at[j],
            device_id=(me, (y + j + 1) % Y), device_id_type=MESH,
        )

    for j in (1, 0, 2):
        d_send[j] = share((y + j + 1) % Y).astype(BF16)
        give(j).start()
    get_inv.wait()
    diag[...] = inv[...] - share(y)
    for j in (0, 2, 1):
        give(j).wait_recv()
        diag[...] -= d_recv[j].astype(F32)
    put_diag = pltpu.make_async_copy(diag, diag_hbm.at[0], out_sem.at[1])
    put_diag.start()

    for h in range(3):
        eighth = 6 * x + 3 * c + h
        group = eighth // 2
        to_y = (3 * z + group // 4 + y) % Y
        for k in range(CORES):
            here = jnp.logical_and(jnp.logical_and(group % 4 == x, to_y == y), c == k)

            @pl.when(jnp.logical_not(here))
            def _():
                pltpu.make_async_copy(s0_send.at[h, k], s0_send.at[h, k], s0_sems.at[2 + 2 * h + k]).wait()

    pltpu.make_async_copy(told, told, st_sems.at[0]).wait()
    passed = tiles.at[pl.ds(0, GROUPS * (Z - 1))]
    pltpu.make_async_copy(passed, passed, ring_send).wait()
    sent = stage.at[pl.ds(0, PLANE - 1)]
    pltpu.make_async_copy(sent, sent, pick_sems.at[0]).wait()
    for j in range(3):
        give(j).wait_send()
    put_off.wait()
    put_diag.wait()


def per_device(ancestors, panels, structure, inverse_diag):
    vmem, smem, dma = pltpu.VMEM, pltpu.SMEM, pltpu.SemaphoreType.DMA
    return pl.pallas_call(
        kernel,
        out_shape=(
            jax.ShapeDtypeStruct((1, 256, 512), BF16),
            jax.ShapeDtypeStruct((1, 128, 512), F32),
        ),
        in_specs=[
            pl.BlockSpec(memory_space=vmem),
            pl.BlockSpec(memory_space=smem),
            pl.BlockSpec(memory_space=pl.ANY),
            pl.BlockSpec(memory_space=pl.ANY),
        ],
        out_specs=(pl.BlockSpec(memory_space=pl.ANY), pl.BlockSpec(memory_space=pl.ANY)),
        scratch_shapes=[
            vmem((1024, 512), BF16),
            vmem((128, 512), F32),
            vmem((3, CORES, 3, 8, 128), F32),
            vmem((GROUPS, 2, 3, 8, 128), F32),
            vmem((8, 128), jnp.int32),
            vmem((X * CORES, 8, 128), jnp.int32),
            smem((X * CORES, 8, 128), jnp.int32),
            vmem((GROUPS * Z, 3, 16, 128), BF16),
            vmem((PLANE, 4, 16, 128), BF16),
            vmem((CORES, Y, X, 4, 16, 128), BF16),
            vmem((256, 1024), BF16),
            vmem((512, 256), BF16),
            vmem((256, 512), BF16),
            vmem((3, 128, 512), BF16),
            vmem((3, 128, 512), BF16),
            vmem((128, 512), F32),
            dma((3,)),
            dma((2,)),
            dma((8,)),
            dma((2,)),
            dma,
            dma((2, Z // 2, GROUPS)),
            dma((2,)),
            dma((3,)),
            dma((3,)),
        ],
        compiler_params=pltpu.CompilerParams(
            collective_id=0, has_side_effects=True, vmem_limit_bytes=32 * 1024 * 1024
        ),
    )(ancestors, structure, panels, inverse_diag)


def solution(mesh):
    return jax.shard_map(
        per_device,
        mesh=mesh,
        in_specs=(P("leaf", "rep"), P("leaf", None, None), P("leaf", None), P("leaf", "rep", None)),
        out_specs=(P("leaf", "rep", None), P("leaf", "rep", None)),
        check_vma=False,
    )
```

time: 250 us -> 68.8 us (0.28)
  waiting for transfers between devices: 210 us -> 0 us
  Pallas kernels: 0 us -> 62.9 us
  between operations: 13.8 us -> 0.65 us
  matrix products: 9.66 us -> 0 us
  local copies, waits for them, and re-layouts: 12 us -> 5 us
  other arithmetic: 3.38 us -> 0 us
    all_gather x1 -> x0, waiting for transfers between devices: 149 us -> none  [per_device(): lax.all_gather(ancestors, 'leaf', axis=0, tiled=True)]
    pallas_call x0 -> x1, Pallas kernels: none -> 62.9 us  [per_device(): pl.pallas_call(kernel, out_shape=(jax.ShapeDtypeStruct((1, 256, 512), BF1...]
    reduce_scatter x2 -> x0, waiting for transfers between devices: 60.4 us -> none  [the longest x1 32.4 us: per_device(): lax.psum_scatter(partial_value, 'rep', scatter_dimension=1, tiled=True)]
    dot_general x3 -> x0, matrix products: 9.66 us -> none  [the longest x1 6.92 us: per_device(): jnp.dot(lax.all_gather(ancestors, 'leaf', axis=0, tiled=True), right_side...]
    neg x1 -> x0, local copies, waits for them, and re-layouts: 6.55 us -> none  [per_device(): -jnp.dot(lax.all_gather(ancestors, 'leaf', axis=0, tiled=True), right_sid...]
    gather x1 -> x0, local copies, waits for them, and re-layouts: 4.86 us -> none  [per_device(): partial_value = gathered[structure, :, child_ids[:, None], :]]
    unnamed x6 -> x10, local copies, waits for them, and re-layouts: 0.44 us -> 5 us
  transfers between devices with their start and end apart: 3 -> 0, of which waited for: 3 -> 0; matrix products, arithmetic and copies ran while one was open for 1% -> 0% of each run, Pallas kernels for 0% -> 0%
where the time goes in v1:
time: 68.8 us; the launch traced here: 68.5 us
  Pallas kernels  62.9 us (91%)
  local copies, waits for them, and re-layouts  5 us (7%)
    pallas_call x1, Pallas kernels, per_device(): pl.pallas_call(kernel, out_shape=(jax.ShapeDtypeStruct((1, 256, 512), BF1...  62.9 us
    unnamed x10, local copies, waits for them, and re-layouts  5 us

profile of v1, /device:TPU:1, one launch (start us, length us, event | category | flops | bytes accessed | tf_op | source)
XLA Modules:
  0.0 68.5 jit_solution(14157573432215089004)
XLA Ops:
  0.6 0.0 copy-start
  0.6 1.2 %copy-done = bf16[1,1024,512]{2,1,0:T(8,128)(2,1)S(1)} copy-done((bf16[1,1024,512]{2,1,0:T(8,128)(2,1)S(1)}, bf16[1,1024,512]{2,1,0:T(8,128)(2,1)}, u32[]{:S(2)}) %copy-start) | copy-done | bytes 1048600
  1.9 0.0 copy-start.1
  1.9 0.9 %copy-done.1 = f32[1,128,512]{2,1,0:T(8,128)S(1)} copy-done((f32[1,128,512]{2,1,0:T(8,128)S(1)}, f32[1,128,512]{2,1,0:T(8,128)}, u32[]{:S(2)}) %copy-start.1) | copy-done | bytes 262168
  2.8 0.0 copy-start.2
  2.8 0.8 %copy-done.2 = bf16[24,768]{1,0:T(8,128)(2,1)S(1)} copy-done((bf16[24,768]{1,0:T(8,128)(2,1)S(1)}, bf16[24,768]{1,0:T(8,128)(2,1)}, u32[]{:S(2)}) %copy-start.2) | copy-done | bytes 36888
  3.6 0.0 copy-start.3
  3.6 0.7 copy-done.3
  4.2 62.9 %shard_map.59 = (bf16[1,256,512]{2,1,0:T(8,128)(2,1)S(1)}, f32[1,128,512]{2,1,0:T(8,128)S(1)}) custom-call(bf16[24,768]{1,0:T(8,128)(2,1)S(1)} %copy-done.2, s32[1,4]{1,0:T(1,128)S(1)} %copy-done.3, bf16[1,1024,512]{2,1,0:T(8,128)(2,1)S(1)} %copy-done, f32[1,128,512]{2,1,0:T(8,128)S(1)} %copy-done.1), custom_call_target="tpu_custom_call" | custom-call | tf_op jit(solution)/shard_map/pallas_call | solution.py:215
  67.1 0.7 %copy.8 = bf16[1,256,512]{2,1,0:T(8,128)(2,1)} copy(bf16[1,256,512]{2,1,0:T(8,128)(2,1)S(1)} %get-tuple-element.4) | data formatting | bytes 524288
  67.8 0.7 %copy.9 = f32[1,128,512]{2,1,0:T(8,128)} copy(f32[1,128,512]{2,1,0:T(8,128)S(1)} %get-tuple-element.5) | data formatting | bytes 524288
Async XLA Ops:
  0.6 1.2 %copy-start = (bf16[1,1024,512]{2,1,0:T(8,128)(2,1)S(1)}, bf16[1,1024,512]{2,1,0:T(8,128)(2,1)}, u32[]{:S(2)}) copy-start(bf16[1,1024,512]{2,1,0:T(8,128)(2,1)} %panels_hbm.1) | copy-start | bytes 3145732
  1.9 0.9 %copy-start.1 = (f32[1,128,512]{2,1,0:T(8,128)S(1)}, f32[1,128,512]{2,1,0:T(8,128)}, u32[]{:S(2)}) copy-start(f32[1,128,512]{2,1,0:T(8,128)} %inv_hbm.1) | copy-start | bytes 786436
  2.8 0.8 %copy-start.2 = (bf16[24,768]{1,0:T(8,128)(2,1)S(1)}, bf16[24,768]{1,0:T(8,128)(2,1)}, u32[]{:S(2)}) copy-start(bf16[24,768]{1,0:T(8,128)(2,1)} %anc_ref.1) | copy-start | bytes 110596
  3.6 0.7 copy-start.3

commit v2 on v1

v2 whole, which is shorter than its diff:
```python
import jax
import jax.numpy as jnp
from jax import lax
from jax.experimental import pallas as pl
from jax.experimental.pallas import tpu as pltpu
from jax.sharding import PartitionSpec as P

MESH = pl.DeviceIdType.MESH
Z, X, Y, CORES = 16, 4, 4, 2
PLANE = X * Y * CORES
GROUPS = 3
JUMPS = (5, -5, 1, -1, 0)
SPREAD = ((1, 1), (-1, -1), (5, 1), (-5, -1), (5, -1), (-5, 1), (5, 3), (2, 1), (-2, -1), (6, 1), (-6, -1))
STEPS = sorted({step for _, step in SPREAD} | {-step for _, step in SPREAD})
assert sorted({j % Z for j in JUMPS} | {(a + b) % Z for a, b in SPREAD}) == list(range(Z))
assert len(JUMPS) + len(SPREAD) == Z
F32, BF16 = jnp.float32, jnp.bfloat16


def kernel(
    anc_hbm, struct_ref, panels_hbm, inv_hbm, off, diag,
    anc, panels, inv, s_send, s_all, pieces, st_send, st_all, st_smem, tiles, stage, picked, lhs, pt,
    d_send, d_recv,
    in_sem, swap_sems, s_sems, spread_send, z_recv, st_sems, pick_sems, d_send_sem, d_recv_sem,
):
    me, y = lax.axis_index("leaf"), lax.axis_index("rep")
    z, x, c = me // 8, (me // 2) % 4, me % 2

    def leaf(zz, xx, cc):
        return (zz * X + xx) * CORES + cc

    def along(step):
        return (z + Z + step) % Z

    get_anc = pltpu.make_async_copy(anc_hbm, anc, in_sem.at[3])
    get_panels = pltpu.make_async_copy(panels_hbm.at[0], panels, in_sem.at[0])
    get_inv = pltpu.make_async_copy(inv_hbm.at[0], inv, in_sem.at[1])
    get_anc.start()
    get_panels.start()
    get_inv.start()

    barrier = pltpu.get_barrier_semaphore()

    def greet(n, carry):
        there = leaf(z, (x + n // 8) % X, (c + n % 2) % CORES)
        pl.semaphore_signal(barrier, inc=1, device_id=(there, (y + n // 2) % Y), device_id_type=MESH)
        return carry

    for jump in JUMPS:
        if jump:
            for e in range(GROUPS):
                from_z, group = along(-jump), 4 * e + x
                there = (leaf(from_z, group // 3, c), (y + 3 * (Z - from_z) + 4 - e) % Y)
                pl.semaphore_signal(barrier, inc=1, device_id=there, device_id_type=MESH)
    for step in STEPS:
        pl.semaphore_signal(barrier, inc=1, device_id=(leaf(along(step), x, c), y), device_id_type=MESH)
    lax.fori_loop(1, PLANE, greet, 0)

    lane = lax.broadcasted_iota(jnp.int32, (8, 128), 1)
    blocks = jnp.zeros((8, 128), jnp.int32)
    for q in range(4):
        blocks = jnp.where(lane == q, struct_ref[0, q], blocks)
    slot = 2 * x + c
    st_send[...] = blocks
    st_all[slot] = blocks
    get_anc.wait()
    rows = anc[...].astype(F32)
    for h in range(3):
        for t in range(3):
            first, second = (rows[8 * h:8 * h + 8, 256 * t + 128 * k:256 * t + 128 * k + 128] for k in range(CORES))
            s_send[h, t] = jnp.where(c == 0, second, first)
            s_all[c, h, t] = jnp.where(c == 0, first, second)

    pl.semaphore_wait(barrier, PLANE - 1 + GROUPS * (len(JUMPS) - 1) + len(STEPS))

    swap = pltpu.make_async_remote_copy(
        src_ref=s_send, dst_ref=s_all.at[c], send_sem=swap_sems.at[0], recv_sem=swap_sems.at[1],
        device_id=(leaf(z, x, 1 - c), y), device_id_type=MESH,
    )
    swap.start()

    def tell(n, carry):
        pltpu.make_async_remote_copy(
            src_ref=st_send, dst_ref=st_all.at[slot], send_sem=st_sems.at[0], recv_sem=st_sems.at[1],
            device_id=(leaf(z, (x + n // 2) % X, (c + n % 2) % CORES), y), device_id_type=MESH,
        ).start()
        return carry

    swap.wait_recv()
    for j in range(3):
        for t in range(3):
            both = [s_all[h // 3, h % 3, t] for h in (2 * j, 2 * j + 1)]
            pieces[j, t] = jnp.concatenate(both, axis=0).astype(BF16)

    def owner(j):
        group = 3 * x + j
        entry = group // 4
        return entry, group % 4, (3 * z + entry + y) % Y

    def scatter(j, jump, here):
        entry, to_x, to_y = owner(j)
        landing = tiles.at[GROUPS * z + entry]
        if here:
            return pltpu.make_async_copy(pieces.at[j], landing, z_recv.at[0, entry])
        return pltpu.make_async_remote_copy(
            src_ref=pieces.at[j], dst_ref=landing,
            send_sem=s_sems.at[0] if jump else s_sems.at[1 + j], recv_sem=z_recv.at[jump % Z, entry],
            device_id=(leaf(along(jump), to_x, c), to_y), device_id_type=MESH,
        )

    def stays(j):
        _, to_x, to_y = owner(j)
        return jnp.logical_and(to_x == x, to_y == y)

    for jump in JUMPS:
        for j in range(3):
            if jump:
                scatter(j, jump, False).start()
            else:
                pl.when(stays(j))(lambda: scatter(j, 0, True).start())
                pl.when(jnp.logical_not(stays(j)))(lambda: scatter(j, 0, False).start())
    lax.fori_loop(1, X * CORES, tell, 0)

    get_panels.wait()
    pt[...] = panels[pl.ds(pl.multiple_of(256 * y, 256), 256), :].T
    told = st_all.at[pl.ds(0, X * CORES - 1)]
    pltpu.make_async_copy(told, told, st_sems.at[1]).wait()
    to_smem = pltpu.make_async_copy(st_all, st_smem, in_sem.at[2])
    to_smem.start()

    landed = set()

    def arrived(o, e):
        if (o, e) not in landed:
            landed.add((o, e))
            pltpu.make_async_copy(tiles.at[0], tiles.at[0], z_recv.at[o % Z, e]).wait()

    def pass_on(o, step, e):
        part = tiles.at[GROUPS * along(-o) + e]
        pltpu.make_async_remote_copy(
            src_ref=part, dst_ref=part, send_sem=spread_send, recv_sem=z_recv.at[(o + step) % Z, e],
            device_id=(leaf(along(step), x, c), y), device_id_type=MESH,
        ).start()

    for o, step in SPREAD:
        for e in range(GROUPS):
            if (o + step) % Z == Z // 2:
                arrived(o, e)
                arrived(-o, e)
                pl.when(c == 0)(lambda: pass_on(o, step, e))
                pl.when(c == 1)(lambda: pass_on(-o, -step, e))
            else:
                arrived(o, e)
                pass_on(o, step, e)
    to_smem.wait()
    for o in range(Z):
        o = o if o < Z // 2 else o - Z
        for e in range(GROUPS):
            arrived(o, e)

    def pick(n, to_x, to_c, to_y):
        child = 2 * to_x + to_c
        row = st_smem[child, 0, to_y]
        for q in range(4):
            column = st_smem[child, 0, q]
            held = 4 * row + lax.rem(y + 4 - lax.div(column, 3), 4)
            stage[n, q] = tiles[held, lax.rem(column, 3)]

    def send(n, carry):
        to_x, to_c, to_y = (x + n // 8) % X, (c + n % 2) % CORES, (y + n // 2) % Y
        pick(n, to_x, to_c, to_y)
        pltpu.make_async_remote_copy(
            src_ref=stage.at[n], dst_ref=picked.at[c, y, x], send_sem=pick_sems.at[0], recv_sem=pick_sems.at[1],
            device_id=(leaf(z, to_x, to_c), to_y), device_id_type=MESH,
        ).start()
        return carry

    lax.fori_loop(1, PLANE, send, 0)
    pick(0, x, c, y)
    pltpu.make_async_copy(stage.at[0], picked.at[c, y, x], pick_sems.at[1]).start()

    pltpu.make_async_copy(picked, picked, pick_sems.at[1]).wait()

    for q in range(4):
        quarter = lax.div(struct_ref[0, q], 3)
        for k in range(CORES):
            for part in range(4):
                rows64 = picked[k, lax.rem(quarter + part, 4), :, q]
                lhs[64 * part:64 * part + 64, 256 * q + 128 * k:256 * q + 128 * k + 128] = rows64.reshape(64, 128)
    off[0] = (-jnp.dot(lhs[...], panels[...], preferred_element_type=F32)).astype(BF16)

    def share(r):
        return jnp.dot(pt[pl.ds(pl.multiple_of(128 * r, 128), 128), :], off[0], preferred_element_type=F32)

    def give(j):
        return pltpu.make_async_remote_copy(
            src_ref=d_send.at[j], dst_ref=d_recv.at[j], send_sem=d_send_sem.at[j], recv_sem=d_recv_sem.at[j],
            device_id=(me, (y + j + 1) % Y), device_id_type=MESH,
        )

    for j in (1, 0, 2):
        d_send[j] = share((y + j + 1) % Y).astype(BF16)
        give(j).start()
    get_inv.wait()
    diag[0] = inv[...] - share(y)
    for j in (0, 2, 1):
        give(j).wait_recv()
        diag[0] -= d_recv[j].astype(F32)

    swap.wait_send()
    pltpu.make_async_copy(told, told, st_sems.at[0]).wait()
    for j in range(3):
        pl.when(jnp.logical_not(stays(j)))(lambda: scatter(j, 0, False).wait_send())
    jumped = tiles.at[pl.ds(0, GROUPS * (len(JUMPS) - 1))]
    pltpu.make_async_copy(jumped, jumped, s_sems.at[0]).wait()
    passed = tiles.at[pl.ds(0, GROUPS * len(SPREAD))]
    pltpu.make_async_copy(passed, passed, spread_send).wait()
    sent = stage.at[pl.ds(0, PLANE - 1)]
    pltpu.make_async_copy(sent, sent, pick_sems.at[0]).wait()
    for j in range(3):
        give(j).wait_send()


def per_device(ancestors, panels, structure, inverse_diag):
    vmem, smem, dma = pltpu.VMEM, pltpu.SMEM, pltpu.SemaphoreType.DMA
    return pl.pallas_call(
        kernel,
        out_shape=(
            pltpu.VMEM((1, 256, 512), BF16),
            pltpu.VMEM((1, 128, 512), F32),
        ),
        in_specs=[
            pl.BlockSpec(memory_space=pl.ANY),
            pl.BlockSpec(memory_space=smem),
            pl.BlockSpec(memory_space=pl.ANY),
            pl.BlockSpec(memory_space=pl.ANY),
        ],
        out_specs=(pl.BlockSpec(memory_space=vmem), pl.BlockSpec(memory_space=vmem)),
        scratch_shapes=[
            vmem((24, 768), BF16),
            vmem((1024, 512), BF16),
            vmem((128, 512), F32),
            vmem((3, 3, 8, 128), F32),
            vmem((CORES, 3, 3, 8, 128), F32),
            vmem((3, 3, 16, 128), BF16),
            vmem((8, 128), jnp.int32),
            vmem((X * CORES, 8, 128), jnp.int32),
            smem((X * CORES, 8, 128), jnp.int32),
            vmem((GROUPS * Z, 3, 16, 128), BF16),
            vmem((PLANE, 4, 16, 128), BF16),
            vmem((CORES, Y, X, 4, 16, 128), BF16),
            vmem((256, 1024), BF16),
            vmem((512, 256), BF16),
            vmem((3, 128, 512), BF16),
            vmem((3, 128, 512), BF16),
            dma((4,)),
            dma((2,)),
            dma((4,)),
            dma,
            dma((Z, GROUPS)),
            dma((2,)),
            dma((2,)),
            dma((3,)),
            dma((3,)),
        ],
        compiler_params=pltpu.CompilerParams(
            collective_id=0, has_side_effects=True, vmem_limit_bytes=32 * 1024 * 1024
        ),
    )(*(pltpu.with_memory_space_constraint(a, pltpu.HBM) for a in (ancestors, structure, panels, inverse_diag)))


def solution(mesh):
    return jax.shard_map(
        per_device,
        mesh=mesh,
        in_specs=(P("leaf", "rep"), P("leaf", None, None), P("leaf", None), P("leaf", "rep", None)),
        out_specs=(P("leaf", "rep", None), P("leaf", "rep", None)),
        check_vma=False,
    )
```

time: 68.8 us -> 56.2 us (0.82)
  Pallas kernels: 62.9 us -> 54 us
  local copies, waits for them, and re-layouts: 5 us -> 1.41 us
    pallas_call x1, Pallas kernels: 62.9 us -> 54 us  [per_device(): pl.pallas_call(kernel, out_shape=(pltpu.VMEM((1, 256, 512), BF16), pltpu....]
    unnamed x10 -> x2, local copies, waits for them, and re-layouts: 5 us -> 1.41 us
where the time goes in v2:
time: 56.2 us; the launch traced here: 56 us
  Pallas kernels  54 us (96%)
  local copies, waits for them, and re-layouts  1.41 us (3%)
  between operations  0.64 us (1%)
    pallas_call x1, Pallas kernels, per_device(): pl.pallas_call(kernel, out_shape=(pltpu.VMEM((1, 256, 512), BF16), pltpu....  54 us
    unnamed x2, local copies, waits for them, and re-layouts  1.41 us

profile of v2, /device:TPU:1, one launch (start us, length us, event | category | flops | bytes accessed | tf_op | source)
XLA Modules:
  0.0 56.0 jit_solution(8635496082208696799)
XLA Ops:
  0.6 54.0 %shard_map.59 = (bf16[1,256,512]{2,1,0:T(8,128)(2,1)S(1)}, f32[1,128,512]{2,1,0:T(8,128)S(1)}) custom-call(bf16[24,768]{1,0:T(8,128)(2,1)} %anc_hbm.1, s32[1,4]{1,0:T(1,128)} %struct_ref.1, bf16[1,1024,512]{2,1,0:T(8,128)(2,1)} %panels_hbm.1, f32[1,128,512]{2,1,0:T(8,128)} %inv_hbm.1), custom_call_target="tpu_custom_call" | custom-call | tf_op jit(solution)/shard_map/pallas_call | solution.py:226
  54.6 0.7 %copy.8 = bf16[1,256,512]{2,1,0:T(8,128)(2,1)} copy(bf16[1,256,512]{2,1,0:T(8,128)(2,1)S(1)} %get-tuple-element.2) | data formatting | bytes 524288
  55.3 0.7 %copy.9 = f32[1,128,512]{2,1,0:T(8,128)} copy(f32[1,128,512]{2,1,0:T(8,128)S(1)} %get-tuple-element.3) | data formatting | bytes 524288

commit v3 on v2

--- a/solution.py
+++ b/solution.py
@@ -9,8 +9,24 @@
 Z, X, Y, CORES = 16, 4, 4, 2
 PLANE = X * Y * CORES
 GROUPS = 3
-JUMPS = (5, -5, 1, -1, 0)
-SPREAD = ((1, 1), (-1, -1), (5, 1), (-5, -1), (5, -1), (-5, 1), (5, 3), (2, 1), (-2, -1), (6, 1), (-6, -1))
+OWNER = (
+    tuple((n // 3, n % 3, n % 3 + 1) for n in range(12)),
+    ((0, 0, 0), (1, 0, 0), (3, 0, 0), (2, 0, 0), (0, 1, 0), (1, 2, 1), (1, 1, 0), (2, 1, 2), (2, 2, 3), (0, 2, 1), (3, 1, 2), (3, 2, 3)),
+    ((0, 0, 2), (0, 1, 3), (3, 0, 0), (1, 0, 2), (1, 1, 3), (2, 0, 0), (2, 1, 1), (3, 1, 1), (1, 2, 0), (2, 2, 0), (3, 2, 0), (0, 2, 0)),
+    tuple((n // 3, n % 3, n % 3 + 1) for n in range(12)),
+)
+SHIFT = ((1, 1, 1, 1), (0, 0, 2, 2), (0, 0, 0, 0))
+PLACE = [[None] * 16 for _ in range(3)]
+HELD = [[[None] * 3 for _ in range(X)] for _ in range(4)]
+for kind in range(4):
+    for n, (at_x, entry, steps) in enumerate(OWNER[kind]):
+        block, row_group = divmod(12 * kind + n, 16)
+        assert block == (3 * kind + entry) // 4 and steps == (3 * kind + entry + SHIFT[block][at_x]) % 4
+        assert HELD[kind][at_x][entry] is None and 4 * steps + at_x not in PLACE[block]
+        PLACE[block][row_group] = 4 * steps + at_x
+        HELD[kind][at_x][entry] = n, steps
+JUMPS = (5, -5, 0)
+SPREAD = ((0, 1), (0, -1), (1, 1), (-1, -1), (5, 1), (-5, -1), (5, -1), (-5, 1), (5, 3), (2, 1), (-2, -1), (6, 1), (-6, -1))
 STEPS = sorted({step for _, step in SPREAD} | {-step for _, step in SPREAD})
 assert sorted({j % Z for j in JUMPS} | {(a + b) % Z for a, b in SPREAD}) == list(range(Z))
 assert len(JUMPS) + len(SPREAD) == Z
@@ -19,9 +35,9 @@
 
 def kernel(
     anc_hbm, struct_ref, panels_hbm, inv_hbm, off, diag,
-    anc, panels, inv, s_send, s_all, pieces, st_send, st_all, st_smem, tiles, stage, picked, lhs, pt,
+    anc, panels, inv, pieces, st_send, st_all, st_smem, tiles, stage, picked, lhs, placed, pt,
     d_send, d_recv,
-    in_sem, swap_sems, s_sems, spread_send, z_recv, st_sems, pick_sems, d_send_sem, d_recv_sem,
+    in_sem, s_sems, spread_send, z_recv, st_sems, pick_sems, d_send_sem, d_recv_sem,
 ):
     me, y = lax.axis_index("leaf"), lax.axis_index("rep")
     z, x, c = me // 8, (me // 2) % 4, me % 2
@@ -31,6 +47,20 @@
 
     def along(step):
         return (z + Z + step) % Z
+
+    def by(index, values):
+        return sum(jnp.where(index == n, value, 0) for n, value in enumerate(values))
+
+    shifts = [by(x, values) for values in SHIFT]
+    owners = by(8 * (z % 4) + 2 * x + c, [
+        sum((1 << 6 * j) * (o[0] + 4 * o[1] + 16 * o[2]) for j, o in enumerate(OWNER[kind][g // 2] for g in range(3 * n, 3 * n + 3)))
+        for kind in range(4) for n in range(X * CORES)
+    ])
+
+    def sources(from_z):
+        return by(4 * (from_z % 4) + x, [
+            sum((1 << 6 * e) * (n + 16 * steps) for e, (n, steps) in enumerate(HELD[kind][at])) for kind in range(4) for at in range(X)
+        ])
 
     get_anc = pltpu.make_async_copy(anc_hbm, anc, in_sem.at[3])
     get_panels = pltpu.make_async_copy(panels_hbm.at[0], panels, in_sem.at[0])
@@ -48,9 +78,10 @@
 
     for jump in JUMPS:
         if jump:
+            held = sources(along(-jump))
             for e in range(GROUPS):
-                from_z, group = along(-jump), 4 * e + x
-                there = (leaf(from_z, group // 3, c), (y + 3 * (Z - from_z) + 4 - e) % Y)
+                pair, steps = held // (1 << 6 * e) % 16, held // (1 << 6 * e + 4) % 4
+                there = (leaf(along(-jump), pair // 3, (2 * pair + c) // 3 % 2), (y + Y - steps) % Y)
                 pl.semaphore_signal(barrier, inc=1, device_id=there, device_id_type=MESH)
     for step in STEPS:
         pl.semaphore_signal(barrier, inc=1, device_id=(leaf(along(step), x, c), y), device_id_type=MESH)
@@ -67,17 +98,10 @@
     rows = anc[...].astype(F32)
     for h in range(3):
         for t in range(3):
-            first, second = (rows[8 * h:8 * h + 8, 256 * t + 128 * k:256 * t + 128 * k + 128] for k in range(CORES))
-            s_send[h, t] = jnp.where(c == 0, second, first)
-            s_all[c, h, t] = jnp.where(c == 0, first, second)
+            halves = [rows[8 * h:8 * h + 8, 256 * t + 128 * k:256 * t + 128 * k + 128] for k in range(2)]
+            pieces[h, t] = jnp.concatenate(halves, axis=0).astype(BF16)
 
     pl.semaphore_wait(barrier, PLANE - 1 + GROUPS * (len(JUMPS) - 1) + len(STEPS))
-
-    swap = pltpu.make_async_remote_copy(
-        src_ref=s_send, dst_ref=s_all.at[c], send_sem=swap_sems.at[0], recv_sem=swap_sems.at[1],
-        device_id=(leaf(z, x, 1 - c), y), device_id_type=MESH,
-    )
-    swap.start()
 
     def tell(n, carry):
         pltpu.make_async_remote_copy(
@@ -86,31 +110,24 @@
         ).start()
         return carry
 
-    swap.wait_recv()
-    for j in range(3):
-        for t in range(3):
-            both = [s_all[h // 3, h % 3, t] for h in (2 * j, 2 * j + 1)]
-            pieces[j, t] = jnp.concatenate(both, axis=0).astype(BF16)
-
     def owner(j):
-        group = 3 * x + j
-        entry = group // 4
-        return entry, group % 4, (3 * z + entry + y) % Y
+        one = owners // (1 << 6 * j) % 64
+        return one // 4 % 4, one % 4, (y + one // 16) % Y, (3 * c + j) % 2
 
     def scatter(j, jump, here):
-        entry, to_x, to_y = owner(j)
+        entry, to_x, to_y, to_c = owner(j)
         landing = tiles.at[GROUPS * z + entry]
         if here:
             return pltpu.make_async_copy(pieces.at[j], landing, z_recv.at[0, entry])
         return pltpu.make_async_remote_copy(
             src_ref=pieces.at[j], dst_ref=landing,
             send_sem=s_sems.at[0] if jump else s_sems.at[1 + j], recv_sem=z_recv.at[jump % Z, entry],
-            device_id=(leaf(along(jump), to_x, c), to_y), device_id_type=MESH,
+            device_id=(leaf(along(jump), to_x, to_c), to_y), device_id_type=MESH,
         )
 
     def stays(j):
-        _, to_x, to_y = owner(j)
-        return jnp.logical_and(to_x == x, to_y == y)
+        _, to_x, to_y, to_c = owner(j)
+        return jnp.logical_and(jnp.logical_and(to_x == x, to_y == y), to_c == c)
 
     for jump in JUMPS:
         for j in range(3):
@@ -120,13 +137,6 @@
                 pl.when(stays(j))(lambda: scatter(j, 0, True).start())
                 pl.when(jnp.logical_not(stays(j)))(lambda: scatter(j, 0, False).start())
     lax.fori_loop(1, X * CORES, tell, 0)
-
-    get_panels.wait()
-    pt[...] = panels[pl.ds(pl.multiple_of(256 * y, 256), 256), :].T
-    told = st_all.at[pl.ds(0, X * CORES - 1)]
-    pltpu.make_async_copy(told, told, st_sems.at[1]).wait()
-    to_smem = pltpu.make_async_copy(st_all, st_smem, in_sem.at[2])
-    to_smem.start()
 
     landed = set()
 
@@ -152,18 +162,25 @@
             else:
                 arrived(o, e)
                 pass_on(o, step, e)
-    to_smem.wait()
+    get_panels.wait()
+    pt[...] = panels[pl.ds(pl.multiple_of(256 * y, 256), 256), :].T
+    told = st_all.at[pl.ds(0, X * CORES - 1)]
+    pltpu.make_async_copy(told, told, st_sems.at[1]).wait()
+    to_smem = pltpu.make_async_copy(st_all, st_smem, in_sem.at[2])
+    to_smem.start()
     for o in range(Z):
         o = o if o < Z // 2 else o - Z
         for e in range(GROUPS):
             arrived(o, e)
+    to_smem.wait()
 
     def pick(n, to_x, to_c, to_y):
         child = 2 * to_x + to_c
         row = st_smem[child, 0, to_y]
+        shift = by(lax.rem(row, 3), shifts)
         for q in range(4):
             column = st_smem[child, 0, q]
-            held = 4 * row + lax.rem(y + 4 - lax.div(column, 3), 4)
+            held = 4 * row + lax.rem(y + 8 - shift - lax.div(column, 3), 4)
             stage[n, q] = tiles[held, lax.rem(column, 3)]
 
     def send(n, carry):
@@ -183,11 +200,18 @@
 
     for q in range(4):
         quarter = lax.div(struct_ref[0, q], 3)
-        for k in range(CORES):
-            for part in range(4):
-                rows64 = picked[k, lax.rem(quarter + part, 4), :, q]
-                lhs[64 * part:64 * part + 64, 256 * q + 128 * k:256 * q + 128 * k + 128] = rows64.reshape(64, 128)
-    off[0] = (-jnp.dot(lhs[...], panels[...], preferred_element_type=F32)).astype(BF16)
+        for part in range(4):
+            pair = [picked[k, lax.rem(quarter + part, 4), :, q].astype(F32).reshape(X, 2, 8, 128) for k in range(CORES)]
+            for k in range(2):
+                rows64 = jnp.concatenate([pair[0][:, k], pair[1][:, k]], axis=1).astype(BF16).reshape(64, 128)
+                lhs[64 * part:64 * part + 64, 256 * q + 128 * k:256 * q + 128 * k + 128] = rows64
+    update = (-jnp.dot(lhs[...], panels[...], preferred_element_type=F32)).astype(BF16)
+    placed[...] = update.reshape(16, 16, 512)
+    kind = lax.rem(by(y, [struct_ref[0, q] for q in range(4)]), 3)
+    for first in range(0, 16, 4):
+        places = by(kind, [sum(PLACE[n][first + m] << 4 * m for m in range(4)) for n in range(3)])
+        for m in range(4):
+            off[0, 16 * (first + m):16 * (first + m) + 16] = placed[lax.rem(lax.div(places, 1 << 4 * m), 16)]
 
     def share(r):
         return jnp.dot(pt[pl.ds(pl.multiple_of(128 * r, 128), 128), :], off[0], preferred_element_type=F32)
@@ -207,7 +231,6 @@
         give(j).wait_recv()
         diag[0] -= d_recv[j].astype(F32)
 
-    swap.wait_send()
     pltpu.make_async_copy(told, told, st_sems.at[0]).wait()
     for j in range(3):
         pl.when(jnp.logical_not(stays(j)))(lambda: scatter(j, 0, False).wait_send())
@@ -240,8 +263,6 @@
             vmem((24, 768), BF16),
             vmem((1024, 512), BF16),
             vmem((128, 512), F32),
-            vmem((3, 3, 8, 128), F32),
-            vmem((CORES, 3, 3, 8, 128), F32),
             vmem((3, 3, 16, 128), BF16),
             vmem((8, 128), jnp.int32),
             vmem((X * CORES, 8, 128), jnp.int32),
@@ -250,11 +271,11 @@
             vmem((PLANE, 4, 16, 128), BF16),
             vmem((CORES, Y, X, 4, 16, 128), BF16),
             vmem((256, 1024), BF16),
+            vmem((16, 16, 512), BF16),
             vmem((512, 256), BF16),
             vmem((3, 128, 512), BF16),
             vmem((3, 128, 512), BF16),
             dma((4,)),
-            dma((2,)),
             dma((4,)),
             dma,
             dma((Z, GROUPS)),

time: 56.2 us -> 53.7 us (0.956)
  Pallas kernels: 54 us -> 51.5 us
    pallas_call x1, Pallas kernels: 54 us -> 51.5 us  [per_device(): pl.pallas_call(kernel, out_shape=(pltpu.VMEM((1, 256, 512), BF16), pltpu....]
where the time goes in v3:
time: 53.7 us; the launch traced here: 53.5 us
  Pallas kernels  51.5 us (96%)
  local copies, waits for them, and re-layouts  1.41 us (3%)
  between operations  0.64 us (1%)
    pallas_call x1, Pallas kernels, per_device(): pl.pallas_call(kernel, out_shape=(pltpu.VMEM((1, 256, 512), BF16), pltpu....  51.5 us
    unnamed x2, local copies, waits for them, and re-layouts  1.41 us

profile of v3, /device:TPU:1, one launch (start us, length us, event | category | flops | bytes accessed | tf_op | source)
XLA Modules:
  0.0 53.5 jit_solution(5893605525160898761)
XLA Ops:
  0.6 51.5 %shard_map.59 = (bf16[1,256,512]{2,1,0:T(8,128)(2,1)S(1)}, f32[1,128,512]{2,1,0:T(8,128)S(1)}) custom-call(bf16[24,768]{1,0:T(8,128)(2,1)} %anc_hbm.1, s32[1,4]{1,0:T(1,128)} %struct_ref.1, bf16[1,1024,512]{2,1,0:T(8,128)(2,1)} %panels_hbm.1, f32[1,128,512]{2,1,0:T(8,128)} %inv_hbm.1), custom_call_target="tpu_custom_call" | custom-call | tf_op jit(solution)/shard_map/pallas_call | solution.py:249
  52.1 0.7 %copy.8 = bf16[1,256,512]{2,1,0:T(8,128)(2,1)} copy(bf16[1,256,512]{2,1,0:T(8,128)(2,1)S(1)} %get-tuple-element.2) | data formatting | bytes 524288
  52.8 0.7 %copy.9 = f32[1,128,512]{2,1,0:T(8,128)} copy(f32[1,128,512]{2,1,0:T(8,128)S(1)} %get-tuple-element.3) | data formatting | bytes 524288

commit v4 on v3

--- a/solution.py
+++ b/solution.py
@@ -25,17 +25,23 @@
         assert HELD[kind][at_x][entry] is None and 4 * steps + at_x not in PLACE[block]
         PLACE[block][row_group] = 4 * steps + at_x
         HELD[kind][at_x][entry] = n, steps
-JUMPS = (5, -5, 0)
-SPREAD = ((0, 1), (0, -1), (1, 1), (-1, -1), (5, 1), (-5, -1), (5, -1), (-5, 1), (5, 3), (2, 1), (-2, -1), (6, 1), (-6, -1))
+JUMPS = (3, -3, 0)
+SPREAD = (
+    (0, 1), (0, -1), (3, 3), (-3, -3), (1, 1), (-1, -1), (3, 1), (-3, -1), (3, 2), (-3, -2), (6, 1), (-6, -1), (6, 2),
+)
 STEPS = sorted({step for _, step in SPREAD} | {-step for _, step in SPREAD})
 assert sorted({j % Z for j in JUMPS} | {(a + b) % Z for a, b in SPREAD}) == list(range(Z))
 assert len(JUMPS) + len(SPREAD) == Z
+TARGETS = sorted(
+    ((dx, dy, dc) for dx in range(X) for dy in range(Y) for dc in range(CORES)),
+    key=lambda d: (-min(d[0], X - d[0]) - min(d[1], Y - d[1]), -d[2], (d[0] + 2 * d[1]) % 4),
+)
 F32, BF16 = jnp.float32, jnp.bfloat16
 
 
 def kernel(
-    anc_hbm, struct_ref, panels_hbm, inv_hbm, off, diag,
-    anc, panels, inv, pieces, st_send, st_all, st_smem, tiles, stage, picked, lhs, placed, pt,
+    anc_hbm, struct_hbm, panels_hbm, inv_hbm, off, diag,
+    struct_ref, anc, panels, inv, pieces, st_send, st_all, st_smem, slots, tiles, stage, picked, lhs, placed, pt,
     d_send, d_recv,
     in_sem, s_sems, spread_send, z_recv, st_sems, pick_sems, d_send_sem, d_recv_sem,
 ):
@@ -65,7 +71,9 @@
     get_anc = pltpu.make_async_copy(anc_hbm, anc, in_sem.at[3])
     get_panels = pltpu.make_async_copy(panels_hbm.at[0], panels, in_sem.at[0])
     get_inv = pltpu.make_async_copy(inv_hbm.at[0], inv, in_sem.at[1])
+    get_struct = pltpu.make_async_copy(struct_hbm, struct_ref, in_sem.at[4])
     get_anc.start()
+    get_struct.start()
     get_panels.start()
     get_inv.start()
 
@@ -87,6 +95,7 @@
         pl.semaphore_signal(barrier, inc=1, device_id=(leaf(along(step), x, c), y), device_id_type=MESH)
     lax.fori_loop(1, PLANE, greet, 0)
 
+    get_struct.wait()
     lane = lax.broadcasted_iota(jnp.int32, (8, 128), 1)
     blocks = jnp.zeros((8, 128), jnp.int32)
     for q in range(4):
@@ -116,7 +125,7 @@
 
     def scatter(j, jump, here):
         entry, to_x, to_y, to_c = owner(j)
-        landing = tiles.at[GROUPS * z + entry]
+        landing = tiles.at[pl.ds(3 * (GROUPS * z + entry), 3)]
         if here:
             return pltpu.make_async_copy(pieces.at[j], landing, z_recv.at[0, entry])
         return pltpu.make_async_remote_copy(
@@ -143,10 +152,10 @@
     def arrived(o, e):
         if (o, e) not in landed:
             landed.add((o, e))
-            pltpu.make_async_copy(tiles.at[0], tiles.at[0], z_recv.at[o % Z, e]).wait()
+            pltpu.make_async_copy(pieces.at[0], pieces.at[0], z_recv.at[o % Z, e]).wait()
 
     def pass_on(o, step, e):
-        part = tiles.at[GROUPS * along(-o) + e]
+        part = tiles.at[pl.ds(3 * (GROUPS * along(-o) + e), 3)]
         pltpu.make_async_remote_copy(
             src_ref=part, dst_ref=part, send_sem=spread_send, recv_sem=z_recv.at[(o + step) % Z, e],
             device_id=(leaf(along(step), x, c), y), device_id_type=MESH,
@@ -168,33 +177,38 @@
     pltpu.make_async_copy(told, told, st_sems.at[1]).wait()
     to_smem = pltpu.make_async_copy(st_all, st_smem, in_sem.at[2])
     to_smem.start()
-    for o in range(Z):
-        o = o if o < Z // 2 else o - Z
-        for e in range(GROUPS):
-            arrived(o, e)
+    def target(n):
+        dx, dy, dc = TARGETS[n]
+        return (x + dx) % X, (y + dy) % Y, (c + dc) % CORES
+
     to_smem.wait()
-
-    def pick(n, to_x, to_c, to_y):
-        child = 2 * to_x + to_c
+    for n in range(PLANE):
+        to_x, to_y, to_c = target(n)
+        child = CORES * to_x + to_c
         row = st_smem[child, 0, to_y]
         shift = by(lax.rem(row, 3), shifts)
         for q in range(4):
             column = st_smem[child, 0, q]
             held = 4 * row + lax.rem(y + 8 - shift - lax.div(column, 3), 4)
-            stage[n, q] = tiles[held, lax.rem(column, 3)]
-
-    def send(n, carry):
-        to_x, to_c, to_y = (x + n // 8) % X, (c + n % 2) % CORES, (y + n // 2) % Y
-        pick(n, to_x, to_c, to_y)
+            slots[n, q] = 3 * held + lax.rem(column, 3)
+    for o in range(Z):
+        o = o if o < Z // 2 else o - Z
+        for e in range(GROUPS):
+            arrived(o, e)
+
+    def pick(n):
+        for q in range(4):
+            stage[n, q] = tiles[slots[n, q]]
+
+    for n in range(PLANE - 1):
+        pick(n)
+        to_x, to_y, to_c = target(n)
         pltpu.make_async_remote_copy(
             src_ref=stage.at[n], dst_ref=picked.at[c, y, x], send_sem=pick_sems.at[0], recv_sem=pick_sems.at[1],
             device_id=(leaf(z, to_x, to_c), to_y), device_id_type=MESH,
         ).start()
-        return carry
-
-    lax.fori_loop(1, PLANE, send, 0)
-    pick(0, x, c, y)
-    pltpu.make_async_copy(stage.at[0], picked.at[c, y, x], pick_sems.at[1]).start()
+    pick(PLANE - 1)
+    pltpu.make_async_copy(stage.at[PLANE - 1], picked.at[c, y, x], pick_sems.at[1]).start()
 
     pltpu.make_async_copy(picked, picked, pick_sems.at[1]).wait()
 
@@ -234,9 +248,9 @@
     pltpu.make_async_copy(told, told, st_sems.at[0]).wait()
     for j in range(3):
         pl.when(jnp.logical_not(stays(j)))(lambda: scatter(j, 0, False).wait_send())
-    jumped = tiles.at[pl.ds(0, GROUPS * (len(JUMPS) - 1))]
+    jumped = tiles.at[pl.ds(0, 3 * GROUPS * (len(JUMPS) - 1))]
     pltpu.make_async_copy(jumped, jumped, s_sems.at[0]).wait()
-    passed = tiles.at[pl.ds(0, GROUPS * len(SPREAD))]
+    passed = tiles.at[pl.ds(0, 3 * GROUPS * len(SPREAD))]
     pltpu.make_async_copy(passed, passed, spread_send).wait()
     sent = stage.at[pl.ds(0, PLANE - 1)]
     pltpu.make_async_copy(sent, sent, pick_sems.at[0]).wait()
@@ -254,12 +268,13 @@
         ),
         in_specs=[
             pl.BlockSpec(memory_space=pl.ANY),
-            pl.BlockSpec(memory_space=smem),
+            pl.BlockSpec(memory_space=pl.ANY),
             pl.BlockSpec(memory_space=pl.ANY),
             pl.BlockSpec(memory_space=pl.ANY),
         ],
         out_specs=(pl.BlockSpec(memory_space=vmem), pl.BlockSpec(memory_space=vmem)),
         scratch_shapes=[
+            smem((1, 4), jnp.int32),
             vmem((24, 768), BF16),
             vmem((1024, 512), BF16),
             vmem((128, 512), F32),
@@ -267,7 +282,8 @@
             vmem((8, 128), jnp.int32),
             vmem((X * CORES, 8, 128), jnp.int32),
             smem((X * CORES, 8, 128), jnp.int32),
-            vmem((GROUPS * Z, 3, 16, 128), BF16),
+            smem((PLANE, 4), jnp.int32),
+            vmem((GROUPS * Z * 3, 16, 128), BF16),
             vmem((PLANE, 4, 16, 128), BF16),
             vmem((CORES, Y, X, 4, 16, 128), BF16),
             vmem((256, 1024), BF16),
@@ -275,7 +291,7 @@
             vmem((512, 256), BF16),
             vmem((3, 128, 512), BF16),
             vmem((3, 128, 512), BF16),
-            dma((4,)),
+            dma((5,)),
             dma((4,)),
             dma,
             dma((Z, GROUPS)),

time: 53.7 us -> 49.9 us (0.929)
  Pallas kernels: 51.5 us -> 47.7 us
    pallas_call x1, Pallas kernels: 51.5 us -> 47.7 us  [per_device(): pl.pallas_call(kernel, out_shape=(pltpu.VMEM((1, 256, 512), BF16), pltpu....]
where the time goes in v4:
time: 49.9 us; the launch traced here: 49.8 us
  Pallas kernels  47.7 us (96%)
  local copies, waits for them, and re-layouts  1.41 us (3%)
  between operations  0.64 us (1%)
    pallas_call x1, Pallas kernels, per_device(): pl.pallas_call(kernel, out_shape=(pltpu.VMEM((1, 256, 512), BF16), pltpu....  47.7 us
    unnamed x2, local copies, waits for them, and re-layouts  1.41 us

profile of v4, /device:TPU:1, one launch (start us, length us, event | category | flops | bytes accessed | tf_op | source)
XLA Modules:
  0.0 49.8 jit_solution(16911827351729905618)
XLA Ops:
  0.6 47.7 %shard_map.59 = (bf16[1,256,512]{2,1,0:T(8,128)(2,1)S(1)}, f32[1,128,512]{2,1,0:T(8,128)S(1)}) custom-call(bf16[24,768]{1,0:T(8,128)(2,1)} %anc_hbm.1, s32[1,4]{1,0:T(1,128)} %struct_hbm.1, bf16[1,1024,512]{2,1,0:T(8,128)(2,1)} %panels_hbm.1, f32[1,128,512]{2,1,0:T(8,128)} %inv_hbm.1), custom_call_target="tpu_custom_call" | custom-call | tf_op jit(solution)/shard_map/pallas_call | solution.py:263
  48.4 0.7 %copy.8 = bf16[1,256,512]{2,1,0:T(8,128)(2,1)} copy(bf16[1,256,512]{2,1,0:T(8,128)(2,1)S(1)} %get-tuple-element.2) | data formatting | bytes 524288
  49.1 0.7 %copy.9 = f32[1,128,512]{2,1,0:T(8,128)} copy(f32[1,128,512]{2,1,0:T(8,128)S(1)} %get-tuple-element.3) | data formatting | bytes 524288

commit v5 on v4

--- a/solution.py
+++ b/solution.py
@@ -34,7 +34,7 @@
 assert len(JUMPS) + len(SPREAD) == Z
 TARGETS = sorted(
     ((dx, dy, dc) for dx in range(X) for dy in range(Y) for dc in range(CORES)),
-    key=lambda d: (-min(d[0], X - d[0]) - min(d[1], Y - d[1]), -d[2], (d[0] + 2 * d[1]) % 4),
+    key=lambda d: (d == (0, 0, 0), -d[2], -min(d[0], X - d[0]) - min(d[1], Y - d[1])),
 )
 F32, BF16 = jnp.float32, jnp.bfloat16
 
@@ -236,7 +236,7 @@
             device_id=(me, (y + j + 1) % Y), device_id_type=MESH,
         )
 
-    for j in (1, 0, 2):
+    for j in (0, 2, 1):
         d_send[j] = share((y + j + 1) % Y).astype(BF16)
         give(j).start()
     get_inv.wait()
@@ -258,9 +258,17 @@
         give(j).wait_send()
 
 
+def write_out(off, diag, off_hbm, diag_hbm, sems):
+    put = [pltpu.make_async_copy(*pair) for pair in ((off, off_hbm, sems.at[0]), (diag, diag_hbm, sems.at[1]))]
+    for copy in put:
+        copy.start()
+    for copy in put:
+        copy.wait()
+
+
 def per_device(ancestors, panels, structure, inverse_diag):
     vmem, smem, dma = pltpu.VMEM, pltpu.SMEM, pltpu.SemaphoreType.DMA
-    return pl.pallas_call(
+    results = pl.pallas_call(
         kernel,
         out_shape=(
             pltpu.VMEM((1, 256, 512), BF16),
@@ -304,6 +312,13 @@
             collective_id=0, has_side_effects=True, vmem_limit_bytes=32 * 1024 * 1024
         ),
     )(*(pltpu.with_memory_space_constraint(a, pltpu.HBM) for a in (ancestors, structure, panels, inverse_diag)))
+    return pl.pallas_call(
+        write_out,
+        out_shape=(pltpu.HBM((1, 256, 512), BF16), pltpu.HBM((1, 128, 512), F32)),
+        in_specs=[pl.BlockSpec(memory_space=vmem)] * 2,
+        out_specs=(pl.BlockSpec(memory_space=pl.ANY),) * 2,
+        scratch_shapes=[dma((2,))],
+    )(*(pltpu.with_memory_space_constraint(a, pltpu.VMEM) for a in results))
 
 
 def solution(mesh):

time: 49.9 us -> 48.4 us (0.970)
  the two profiles are of different devices: /device:TPU:1 before, /device:TPU:64 now
where the time goes in v5:
time: 48.4 us; the launch traced here: 48.3 us
  Pallas kernels  47.7 us (99%)
  between operations  0.64 us (1%)
    pallas_call x1, Pallas kernels, per_device(): pl.pallas_call(kernel, out_shape=(pltpu.VMEM((1, 256, 512), BF16), pltpu....  46.9 us

profile of v5, /device:TPU:64, one launch (start us, length us, event | category | flops | bytes accessed | tf_op | source)
XLA Modules:
  0.0 48.3 jit_solution(15192645754026167689)
XLA Ops:
  0.6 46.9 %shard_map.59 = (bf16[1,256,512]{2,1,0:T(8,128)(2,1)S(1)}, f32[1,128,512]{2,1,0:T(8,128)S(1)}) custom-call(bf16[24,768]{1,0:T(8,128)(2,1)} %anc_hbm.1, s32[1,4]{1,0:T(1,128)} %struct_hbm.1, bf16[1,1024,512]{2,1,0:T(8,128)(2,1)} %panels_hbm.1, f32[1,128,512]{2,1,0:T(8,128)} %inv_hbm.1), custom_call_target="tpu_custom_call" | custom-call | tf_op jit(solution)/shard_map/pallas_call | solution.py:271
  47.5 0.8 %shard_map.60 = (bf16[1,256,512]{2,1,0:T(8,128)(2,1)}, f32[1,128,512]{2,1,0:T(8,128)}) custom-call(bf16[1,256,512]{2,1,0:T(8,128)(2,1)S(1)} %get-tuple-element.4.off, f32[1,128,512]{2,1,0:T(8,128)S(1)} %get-tuple-element.5.diag), custom_call_target="tpu_custom_call" | custom-call | tf_op jit(solution)/shard_map/pallas_call | solution.py:315

commit v6 on v5

--- a/solution.py
+++ b/solution.py
@@ -227,22 +227,27 @@
         for m in range(4):
             off[0, 16 * (first + m):16 * (first + m) + 16] = placed[lax.rem(lax.div(places, 1 << 4 * m), 16)]
 
-    def share(r):
-        return jnp.dot(pt[pl.ds(pl.multiple_of(128 * r, 128), 128), :], off[0], preferred_element_type=F32)
-
-    def give(j):
+    def share(row, count):
+        return jnp.dot(pt[pl.ds(pl.multiple_of(row, count), count), :], off[0], preferred_element_type=F32)
+
+    def give(j, half):
+        rows = pl.ds(64 * half, 64)
         return pltpu.make_async_remote_copy(
-            src_ref=d_send.at[j], dst_ref=d_recv.at[j], send_sem=d_send_sem.at[j], recv_sem=d_recv_sem.at[j],
+            src_ref=d_send.at[j, rows], dst_ref=d_recv.at[j, rows],
+            send_sem=d_send_sem.at[j, half], recv_sem=d_recv_sem.at[j, half],
             device_id=(me, (y + j + 1) % Y), device_id_type=MESH,
         )
 
+    for half in range(2):
+        for j in (1, 0, 2):
+            row = 128 * ((y + j + 1) % Y) + 64 * half
+            d_send[j, 64 * half:64 * half + 64] = share(row, 64).astype(BF16)
+            give(j, half).start()
+    get_inv.wait()
+    diag[0] = inv[...] - share(128 * y, 128)
     for j in (0, 2, 1):
-        d_send[j] = share((y + j + 1) % Y).astype(BF16)
-        give(j).start()
-    get_inv.wait()
-    diag[0] = inv[...] - share(y)
-    for j in (0, 2, 1):
-        give(j).wait_recv()
+        for half in range(2):
+            give(j, half).wait_recv()
         diag[0] -= d_recv[j].astype(F32)
 
     pltpu.make_async_copy(told, told, st_sems.at[0]).wait()
@@ -255,7 +260,8 @@
     sent = stage.at[pl.ds(0, PLANE - 1)]
     pltpu.make_async_copy(sent, sent, pick_sems.at[0]).wait()
     for j in range(3):
-        give(j).wait_send()
+        for half in range(2):
+            give(j, half).wait_send()
 
 
 def write_out(off, diag, off_hbm, diag_hbm, sems):
@@ -305,8 +311,8 @@
             dma((Z, GROUPS)),
             dma((2,)),
             dma((2,)),
-            dma((3,)),
-            dma((3,)),
+            dma((3, 2)),
+            dma((3, 2)),
         ],
         compiler_params=pltpu.CompilerParams(
             collective_id=0, has_side_effects=True, vmem_limit_bytes=32 * 1024 * 1024

time: 48.4 us -> 47.9 us (0.990)
  the two profiles are of different devices: /device:TPU:64 before, /device:TPU:1 now
where the time goes in v6:
time: 47.9 us; the launch traced here: 47.8 us
  Pallas kernels  47.1 us (98%)
  between operations  0.64 us (1%)
    pallas_call x1, Pallas kernels, per_device(): pl.pallas_call(kernel, out_shape=(pltpu.VMEM((1, 256, 512), BF16), pltpu....  46.3 us

profile of v6, /device:TPU:1, one launch (start us, length us, event | category | flops | bytes accessed | tf_op | source)
XLA Modules:
  0.0 47.8 jit_solution(11132163023930405751)
XLA Ops:
  0.6 46.3 %shard_map.59 = (bf16[1,256,512]{2,1,0:T(8,128)(2,1)S(1)}, f32[1,128,512]{2,1,0:T(8,128)S(1)}) custom-call(bf16[24,768]{1,0:T(8,128)(2,1)} %anc_hbm.1, s32[1,4]{1,0:T(1,128)} %struct_hbm.1, bf16[1,1024,512]{2,1,0:T(8,128)(2,1)} %panels_hbm.1, f32[1,128,512]{2,1,0:T(8,128)} %inv_hbm.1), custom_call_target="tpu_custom_call" | custom-call | tf_op jit(solution)/shard_map/pallas_call | solution.py:277
  46.9 0.8 %shard_map.60 = (bf16[1,256,512]{2,1,0:T(8,128)(2,1)}, f32[1,128,512]{2,1,0:T(8,128)}) custom-call(bf16[1,256,512]{2,1,0:T(8,128)(2,1)S(1)} %get-tuple-element.4.off, f32[1,128,512]{2,1,0:T(8,128)S(1)} %get-tuple-element.5.diag), custom_call_target="tpu_custom_call" | custom-call | tf_op jit(solution)/shard_map/pallas_call | solution.py:321

commit v7 on v6

--- a/solution.py
+++ b/solution.py
@@ -40,8 +40,8 @@
 
 
 def kernel(
-    anc_hbm, struct_hbm, panels_hbm, inv_hbm, off, diag,
-    struct_ref, anc, panels, inv, pieces, st_send, st_all, st_smem, slots, tiles, stage, picked, lhs, placed, pt,
+    anc, struct_hbm, panels_hbm, inv_hbm, off, diag,
+    struct_ref, panels, inv, pieces, st_send, st_all, st_smem, slots, tiles, stage, picked, lhs, placed, pt,
     d_send, d_recv,
     in_sem, s_sems, spread_send, z_recv, st_sems, pick_sems, d_send_sem, d_recv_sem,
 ):
@@ -68,11 +68,9 @@
             sum((1 << 6 * e) * (n + 16 * steps) for e, (n, steps) in enumerate(HELD[kind][at])) for kind in range(4) for at in range(X)
         ])
 
-    get_anc = pltpu.make_async_copy(anc_hbm, anc, in_sem.at[3])
     get_panels = pltpu.make_async_copy(panels_hbm.at[0], panels, in_sem.at[0])
     get_inv = pltpu.make_async_copy(inv_hbm.at[0], inv, in_sem.at[1])
-    get_struct = pltpu.make_async_copy(struct_hbm, struct_ref, in_sem.at[4])
-    get_anc.start()
+    get_struct = pltpu.make_async_copy(struct_hbm, struct_ref, in_sem.at[3])
     get_struct.start()
     get_panels.start()
     get_inv.start()
@@ -103,7 +101,6 @@
     slot = 2 * x + c
     st_send[...] = blocks
     st_all[slot] = blocks
-    get_anc.wait()
     rows = anc[...].astype(F32)
     for h in range(3):
         for t in range(3):
@@ -281,7 +278,7 @@
             pltpu.VMEM((1, 128, 512), F32),
         ),
         in_specs=[
-            pl.BlockSpec(memory_space=pl.ANY),
+            pl.BlockSpec(memory_space=vmem),
             pl.BlockSpec(memory_space=pl.ANY),
             pl.BlockSpec(memory_space=pl.ANY),
             pl.BlockSpec(memory_space=pl.ANY),
@@ -289,7 +286,6 @@
         out_specs=(pl.BlockSpec(memory_space=vmem), pl.BlockSpec(memory_space=vmem)),
         scratch_shapes=[
             smem((1, 4), jnp.int32),
-            vmem((24, 768), BF16),
             vmem((1024, 512), BF16),
             vmem((128, 512), F32),
             vmem((3, 3, 16, 128), BF16),
@@ -305,7 +301,7 @@
             vmem((512, 256), BF16),
             vmem((3, 128, 512), BF16),
             vmem((3, 128, 512), BF16),
-            dma((5,)),
+            dma((4,)),
             dma((4,)),
             dma,
             dma((Z, GROUPS)),
@@ -317,7 +313,7 @@
         compiler_params=pltpu.CompilerParams(
             collective_id=0, has_side_effects=True, vmem_limit_bytes=32 * 1024 * 1024
         ),
-    )(*(pltpu.with_memory_space_constraint(a, pltpu.HBM) for a in (ancestors, structure, panels, inverse_diag)))
+    )(ancestors, *(pltpu.with_memory_space_constraint(a, pltpu.HBM) for a in (structure, panels, inverse_diag)))
     return pl.pallas_call(
         write_out,
         out_shape=(pltpu.HBM((1, 256, 512), BF16), pltpu.HBM((1, 128, 512), F32)),

time: 47.9 us -> 48.7 us (1.017)
  local copies, waits for them, and re-layouts: 0 us -> 0.76 us
    unnamed x0 -> x2, local copies, waits for them, and re-layouts: none -> 0.76 us
where the time goes in v7:
time: 48.7 us; the launch traced here: 48.5 us
  Pallas kernels  47.1 us (97%)
  local copies, waits for them, and re-layouts  0.76 us (2%)
  between operations  0.65 us (1%)
    pallas_call x1, Pallas kernels, per_device(): pl.pallas_call(kernel, out_shape=(pltpu.VMEM((1, 256, 512), BF16), pltpu....  46.3 us

profile of v7, /device:TPU:1, one launch (start us, length us, event | category | flops | bytes accessed | tf_op | source)
XLA Modules:
  0.0 48.5 jit_solution(2035822926685872696)
XLA Ops:
  0.6 0.0 copy-start
  0.6 0.8 %copy-done = bf16[24,768]{1,0:T(8,128)(2,1)S(1)} copy-done((bf16[24,768]{1,0:T(8,128)(2,1)S(1)}, bf16[24,768]{1,0:T(8,128)(2,1)}, u32[]{:S(2)}) %copy-start) | copy-done | bytes 36888
  1.4 46.3 %shard_map.59 = (bf16[1,256,512]{2,1,0:T(8,128)(2,1)S(1)}, f32[1,128,512]{2,1,0:T(8,128)S(1)}) custom-call(bf16[24,768]{1,0:T(8,128)(2,1)S(1)} %copy-done, s32[1,4]{1,0:T(1,128)} %struct_hbm.1, bf16[1,1024,512]{2,1,0:T(8,128)(2,1)} %panels_hbm.1, f32[1,128,512]{2,1,0:T(8,128)} %inv_hbm.1), custom_call_target="tpu_custom_call" | custom-call | tf_op jit(solution)/shard_map/pallas_call | solution.py:274
  47.7 0.8 %shard_map.60 = (bf16[1,256,512]{2,1,0:T(8,128)(2,1)}, f32[1,128,512]{2,1,0:T(8,128)}) custom-call(bf16[1,256,512]{2,1,0:T(8,128)(2,1)S(1)} %get-tuple-element.4.off, f32[1,128,512]{2,1,0:T(8,128)S(1)} %get-tuple-element.5.diag), custom_call_target="tpu_custom_call" | custom-call | tf_op jit(solution)/shard_map/pallas_call | solution.py:317
Async XLA Ops:
  0.6 0.8 %copy-start = (bf16[24,768]{1,0:T(8,128)(2,1)S(1)}, bf16[24,768]{1,0:T(8,128)(2,1)}, u32[]{:S(2)}) copy-start(bf16[24,768]{1,0:T(8,128)(2,1)} %anc.1) | copy-start | bytes 110596

commit v8 on v6

--- a/solution.py
+++ b/solution.py
@@ -41,7 +41,7 @@
 
 def kernel(
     anc_hbm, struct_hbm, panels_hbm, inv_hbm, off, diag,
-    struct_ref, anc, panels, inv, pieces, st_send, st_all, st_smem, slots, tiles, stage, picked, lhs, placed, pt,
+    struct_ref, panels, inv, pieces, st_send, st_all, st_smem, slots, tiles, stage, picked, lhs, placed, pt,
     d_send, d_recv,
     in_sem, s_sems, spread_send, z_recv, st_sems, pick_sems, d_send_sem, d_recv_sem,
 ):
@@ -68,7 +68,7 @@
             sum((1 << 6 * e) * (n + 16 * steps) for e, (n, steps) in enumerate(HELD[kind][at])) for kind in range(4) for at in range(X)
         ])
 
-    get_anc = pltpu.make_async_copy(anc_hbm, anc, in_sem.at[3])
+    get_anc = pltpu.make_async_copy(anc_hbm, pieces, in_sem.at[3])
     get_panels = pltpu.make_async_copy(panels_hbm.at[0], panels, in_sem.at[0])
     get_inv = pltpu.make_async_copy(inv_hbm.at[0], inv, in_sem.at[1])
     get_struct = pltpu.make_async_copy(struct_hbm, struct_ref, in_sem.at[4])
@@ -104,12 +104,6 @@
     st_send[...] = blocks
     st_all[slot] = blocks
     get_anc.wait()
-    rows = anc[...].astype(F32)
-    for h in range(3):
-        for t in range(3):
-            halves = [rows[8 * h:8 * h + 8, 256 * t + 128 * k:256 * t + 128 * k + 128] for k in range(2)]
-            pieces[h, t] = jnp.concatenate(halves, axis=0).astype(BF16)
-
     pl.semaphore_wait(barrier, PLANE - 1 + GROUPS * (len(JUMPS) - 1) + len(STEPS))
 
     def tell(n, carry):
@@ -274,6 +268,7 @@
 
 def per_device(ancestors, panels, structure, inverse_diag):
     vmem, smem, dma = pltpu.VMEM, pltpu.SMEM, pltpu.SemaphoreType.DMA
+    pieces = ancestors.reshape(3, 8, 3, 2, 128).transpose(0, 2, 3, 1, 4).reshape(3, 3, 16, 128)
     results = pl.pallas_call(
         kernel,
         out_shape=(
@@ -289,7 +284,6 @@
         out_specs=(pl.BlockSpec(memory_space=vmem), pl.BlockSpec(memory_space=vmem)),
         scratch_shapes=[
             smem((1, 4), jnp.int32),
-            vmem((24, 768), BF16),
             vmem((1024, 512), BF16),
             vmem((128, 512), F32),
             vmem((3, 3, 16, 128), BF16),
@@ -317,7 +311,7 @@
         compiler_params=pltpu.CompilerParams(
             collective_id=0, has_side_effects=True, vmem_limit_bytes=32 * 1024 * 1024
         ),
-    )(*(pltpu.with_memory_space_constraint(a, pltpu.HBM) for a in (ancestors, structure, panels, inverse_diag)))
+    )(*(pltpu.with_memory_space_constraint(a, pltpu.HBM) for a in (pieces, structure, panels, inverse_diag)))
     return pl.pallas_call(
         write_out,
         out_shape=(pltpu.HBM((1, 256, 512), BF16), pltpu.HBM((1, 128, 512), F32)),

time: 47.9 us -> 47.9 us (level)
  no operation moved by 1% of the time
where the time goes in v8:
time: 47.9 us; the launch traced here: 47.7 us
  Pallas kernels  47.1 us (98%)
  between operations  0.64 us (1%)
    pallas_call x1, Pallas kernels, per_device(): pl.pallas_call(kernel, out_shape=(pltpu.VMEM((1, 256, 512), BF16), pltpu....  46.3 us

profile of v8, /device:TPU:1, one launch (start us, length us, event | category | flops | bytes accessed | tf_op | source)
XLA Modules:
  0.0 47.7 jit_solution(17685275997406536821)
XLA Ops:
  0.6 46.3 %shard_map.59 = (bf16[1,256,512]{2,1,0:T(8,128)(2,1)S(1)}, f32[1,128,512]{2,1,0:T(8,128)S(1)}) custom-call(bf16[3,3,16,128]{3,2,1,0:T(8,128)(2,1)} %bitcast.5, s32[1,4]{1,0:T(1,128)} %struct_hbm.1, bf16[1,1024,512]{2,1,0:T(8,128)(2,1)} %panels_hbm.1, f32[1,128,512]{2,1,0:T(8,128)} %inv_hbm.1), custom_call_target="tpu_custom_call" | custom-call | tf_op jit(solution)/shard_map/pallas_call | solution.py:272
  46.9 0.8 %shard_map.60 = (bf16[1,256,512]{2,1,0:T(8,128)(2,1)}, f32[1,128,512]{2,1,0:T(8,128)}) custom-call(bf16[1,256,512]{2,1,0:T(8,128)(2,1)S(1)} %get-tuple-element.4.off, f32[1,128,512]{2,1,0:T(8,128)S(1)} %get-tuple-element.5.diag), custom_call_target="tpu_custom_call" | custom-call | tf_op jit(solution)/shard_map/pallas_call | solution.py:315
